TPU v7x, 128 devices: a whole 4x4x4 slice. The times are simulated.
128 devices in a mesh: dp: 16 (over x, y_hi, core), tensor: 8 (over y_lo, z).
Axes of the slice: x: 4, y: 4 (y_hi: 2, y_lo: 2; y = y_hi * 2 + y_lo), z: 4, core: 2. Of those that a mesh axis runs over, the one named last changes fastest.
Arguments:
- student_in: bfloat16 [16384, 4096], P(('dp', 'tensor')), may hold values from -24 to 24
- norm_gain: float32 [4096], replicated, may hold values from 0.5 to 1.5
- w_query: bfloat16 [4096, 4096], P(None, 'tensor'), may hold values from -0.09375 to 0.09375
- w_key: bfloat16 [4096, 1024], P(None, 'tensor'), may hold values from -2.90625 to 2.90625
- w_value: bfloat16 [4096, 1024], P(None, 'tensor'), may hold values from -0.09375 to 0.09375
- w_out: bfloat16 [4096, 4096], P('tensor'), may hold values from -0.09375 to 0.09375
- projection: bfloat16 [4096, 8192], P(None, 'tensor'), may hold values from -0.09375 to 0.09375
- teacher_rows: bfloat16 [16384, 8192], P('dp', 'tensor'), may hold values from -6 to 6
- lengths: int32 [16], P('dp'), may hold values from 256 to 1024, as said below
Outputs:
- proj_grad: float32 [4096, 8192], P('dp', 'tensor')
- seq_loss: float32 [16], P('dp')
Inputs may be any that keep to these rules, and one draw needn't show every extreme that they name: `lengths`: at least one sequence is valid over all 1024 positions.
All inputs are finite; a program needn't handle non-finite values.
Results may differ from a plain program's by a relative error of at most 0.017.
Values may be sent and summed in bfloat16 or wider, within the bound.
No kernel may reach another device: no remote copies, remote signals or barrier semaphores. Data moves between devices by JAX's collectives and lax.ppermute only.
A program may use at most 128 MiB of HBM per device.

v0:
```python
import math

import jax
import jax.numpy as jnp
from jax import lax
from jax.sharding import PartitionSpec as P

HEAD_DIM = 128
DT = 8192


EPSILON = 1e-05
ROPE_BASE = 500000.0
NEG_LARGE = -1e30


def root_norm(inputs, norm_gain):
    widened = inputs.astype(jnp.float32)
    mean_square = jnp.mean(widened * widened, axis=-1, keepdims=True)
    return (widened * lax.rsqrt(mean_square + EPSILON) * norm_gain).astype(jnp.bfloat16)


def rotate(values):
    seq_len = values.shape[0]
    half_dim = HEAD_DIM // 2
    positions = jnp.arange(seq_len).astype(jnp.float32)[:, None]
    inverse = ROPE_BASE ** (-2.0 * jnp.arange(half_dim).astype(jnp.float32) / HEAD_DIM)
    angles = (positions * inverse)[:, None, :]
    cosine = jnp.cos(angles)
    sine_part = jnp.sin(angles)
    heads_view = values.reshape(seq_len, -1, HEAD_DIM)
    lower_half = heads_view[..., :half_dim]
    upper_half = heads_view[..., half_dim:]
    turned = jnp.concatenate(
        [
            lower_half * cosine - upper_half * sine_part,
            upper_half * cosine + lower_half * sine_part,
        ],
        axis=-1,
    )
    return turned.reshape(seq_len, -1).astype(jnp.bfloat16)


def attend(queries, keys_all, values_all, length):
    seq_len = queries.shape[0]
    kv_count = keys_all.shape[1] // HEAD_DIM
    group_size = queries.shape[1] // HEAD_DIM // kv_count
    block_len = min(512, seq_len)
    factor = 1.0 / math.sqrt(HEAD_DIM)
    outputs = []
    for number in range(seq_len // block_len):
        key_end = (number + 1) * block_len
        query_block = queries[number * block_len : key_end].reshape(
            block_len, kv_count, group_size, HEAD_DIM
        )
        key_block = keys_all[:key_end].reshape(key_end, kv_count, HEAD_DIM)
        value_block = values_all[:key_end].reshape(key_end, kv_count, HEAD_DIM)
        scores = (
            jnp.einsum("qhgd,khd->hgqk", query_block, key_block, preferred_element_type=jnp.float32)
            * factor
        )
        query_pos = number * block_len + jnp.arange(block_len)
        key_pos = jnp.arange(key_end)
        allowed = (query_pos[:, None] >= key_pos[None, :]) & (key_pos[None, :] < length)
        scores = jnp.where(allowed, scores, NEG_LARGE)
        highest = jnp.max(scores, axis=-1, keepdims=True)
        weights = jnp.exp(scores - highest)
        weights_low = (weights / jnp.sum(weights, axis=-1, keepdims=True)).astype(jnp.bfloat16)
        blended = jnp.einsum(
            "hgqk,khd->qhgd", weights_low, value_block, preferred_element_type=jnp.float32
        )
        outputs.append(blended.astype(jnp.bfloat16).reshape(block_len, -1))
    return jnp.concatenate(outputs, axis=0)


def shards(
    student_in, norm_gain, w_query, w_key, w_value, w_out, projection, teacher_rows, lengths
):
    gathered = lax.all_gather(student_in, "tensor", axis=0, tiled=True)
    normed = root_norm(gathered, norm_gain)
    queries = rotate(jnp.dot(normed, w_query, preferred_element_type=jnp.float32))
    keys_all = rotate(jnp.dot(normed, w_key, preferred_element_type=jnp.float32))
    values_all = jnp.dot(normed, w_value, preferred_element_type=jnp.float32).astype(jnp.bfloat16)
    length = lengths[0]
    attended = attend(queries, keys_all, values_all, length)
    own_sum = lax.psum_scatter(
        jnp.dot(attended, w_out, preferred_element_type=jnp.float32).astype(jnp.bfloat16),
        "tensor",
        scatter_dimension=0,
        tiled=True,
    ).astype(jnp.float32)
    own_layer = (student_in.astype(jnp.float32) + own_sum).astype(jnp.bfloat16)
    layer = lax.all_gather(own_layer, "tensor", axis=0, tiled=True)
    predicted = jnp.dot(layer, projection, preferred_element_type=jnp.float32)
    seq_len = layer.shape[0]
    live = (jnp.arange(seq_len) < length)[:, None]
    residue = jnp.where(live, predicted - teacher_rows.astype(jnp.float32), jnp.float32(0.0))
    squared = lax.psum(jnp.sum(residue * residue), "tensor")
    seq_loss = squared / (lengths.astype(jnp.float32) * DT)
    error_grad = (residue / length.astype(jnp.float32)).astype(jnp.bfloat16)
    proj_grad = lax.psum_scatter(
        lax.dot_general(
            layer, error_grad, (((0,), (0,)), ((), ())), preferred_element_type=jnp.float32
        ).astype(jnp.bfloat16),
        "dp",
        scatter_dimension=0,
        tiled=True,
    ).astype(jnp.float32)
    return (proj_grad, seq_loss)


def solution(mesh):
    placed = (
        P(("dp", "tensor"), None),
        P(),
        P(None, "tensor"),
        P(None, "tensor"),
        P(None, "tensor"),
        P("tensor", None),
        P(None, "tensor"),
        P("dp", "tensor"),
        P("dp"),
    )
    return jax.shard_map(
        shards, mesh=mesh, in_specs=placed, out_specs=(P("dp", "tensor"), P("dp")), check_vma=False
    )
```

profile of v0, /device:TPU:0, one launch (start us, length us, event | category | flops | bytes accessed | tf_op | source)
XLA Modules:
  0.0 485.7 jit_solution(13475884402678130589)
XLA Ops:
  10.0 3.0 multiply_cosine_fusion
  13.0 91.2 %all-gather.3.cloned.1.call-done = bf16[1024,4096]{1,0:T(8,128)(2,1)} async-done(((bf16[128,4096]{1,0:T(8,128)(2,1)}), bf16[1024,4096]{1,0:T(8,128)(2,1)}) %all-gather.3.cloned.1.call-update) | async-done | bytes 8388624 | tf_op jit(solution)/shard_map/all_gather | solution.py:79
  104.3 5.1 %fusion = f32[1024]{0:T(1024)S(1)} fusion(bf16[1024,4096]{1,0:T(8,128)(2,1)} %all-gather.3.cloned.1.call-done), kind=kLoop, calls=%fused_computation.2 | loop fusion | flops 12581888 | bytes 8392704 | tf_op jit(solution)/shard_map/reduce_sum | solution.py:19
  109.4 10.3 %fusion.2 = bf16[1024,4096]{1,0:T(8,128)(2,1)} fusion(bf16[1024,4096]{1,0:T(8,128)(2,1)} %all-gather.3.cloned.1.call-done, f32[4096]{0:T(1024)S(1)} %copy-done.7, f32[1024]{0:T(1024)S(1)} %add_rsqrt_fusion), kind=kLoop, calls=%fused_computation.4 | loop fusion | flops 16777216 | bytes 16797696 | tf_op jit(solution)/shard_map/convert_element_type | solution.py:20
  119.7 6.6 %convolution_convert_fusion.2 = bf16[1024,128]{1,0:T(8,128)(2,1)} fusion(bf16[1024,4096]{1,0:T(8,128)(2,1)} %fusion.2, bf16[4096,128]{1,0:T(8,128)(2,1)S(1)} %copy-done), kind=kOutput, calls=%fused_computation.36 | convolution fusion | flops 1073872896 | bytes 9699328 | tf_op jit(solution)/shard_map/dot_general | solution.py:83
  126.3 2.9 convolution_bitcast_fusion
  129.2 6.5 %fusion.54 = f32[1024,512]{0,1:T(8,128)S(1)} fusion(bf16[1024,4096]{1,0:T(8,128)(2,1)S(1)} %copy-done.2, bf16[4096,512]{1,0:T(8,128)(2,1)} %param.11), kind=kOutput, calls=%fused_computation.84 | convolution fusion | flops 4294967296 | bytes 14680064 | tf_op jit(solution)/shard_map/dot_general | solution.py:81
  135.7 2.0 fusion.36
  138.9 1.8 copy.30
  140.7 1.9 copy.29
  142.6 2.4 subtract_convert_fusion
  147.2 1.4 fusion.19
  148.6 2.0 fusion.4
  150.6 1.8 fusion.3
  152.5 2.7 fusion.16
  155.2 6.9 %convolution_convert_fusion.1 = bf16[1024,4096]{1,0:T(8,128)(2,1)} fusion(bf16[512,4096]{1,0:T(8,128)(2,1)S(1)} %copy-done.9, bf16[512,512]{0,1:T(8,128)(2,1)S(1)} %bitcast.92, bf16[512,512]{0,1:T(8,128)(2,1)S(1)} %bitcast.91), kind=kOutput, calls=%fused_computation.9 | convolution fusion | flops 4301258752 | bytes 13631488 | tf_op jit(solution)/shard_map/dot_general | solution.py:87
  162.2 91.6 %reduce-scatter.3.cloned.1.call-done = bf16[128,4096]{1,0:T(8,128)(2,1)} async-done(((bf16[1024,4096]{1,0:T(8,128)(2,1)}), bf16[128,4096]{1,0:T(8,128)(2,1)}) %reduce-scatter.3.cloned.1.call-update) | async-done | bytes 1048592 | tf_op jit(solution)/shard_map/reduce_scatter | solution.py:86
  253.8 2.4 add_convert_fusion
  256.3 90.9 %all-gather.5.cloned.1.call-done = bf16[1024,4096]{1,0:T(8,128)(2,1)} async-done(((bf16[128,4096]{1,0:T(8,128)(2,1)}), bf16[1024,4096]{1,0:T(8,128)(2,1)}) %all-gather.5.cloned.1.call-update) | async-done | bytes 8388624 | tf_op jit(solution)/shard_map/all_gather | solution.py:93
  347.2 15.0 %multiply_reduce_fusion = (f32[]{:T(128)}, f32[1024,1024]{1,0:T(8,128)S(1)}) fusion(bf16[1024,1024]{1,0:T(8,128)(2,1)S(1)} %copy-done.10, pred[1024]{0:T(1024)(128)(4,1)S(1)} %iota_compare_fusion.2, bf16[1024,4096]{1,0:T(8,128)(2,1)} %all-gather.5.cloned.1.call-done, bf16[4096,1024]{1,0:T(8,128)(2,1)} %param.15), kind=kOutput, calls=%fused_computation.15 | convolution fusion | flops 8595177472 | bytes 23069700 | tf_op jit(solution)/shard_map/dot_general | solution.py:94
  362.2 12.4 %convolution_convert_fusion = bf16[4096,1024]{1,0:T(8,128)(2,1)} fusion(bf16[1024,4096]{1,0:T(8,128)(2,1)S(1)} %copy-done.8, f32[1024,1024]{1,0:T(8,128)S(1)} %get-tuple-element.15, bf16[1024,1024]{1,0:T(8,128)(2,1)S(1)} %copy-done.10, f32[]{:T(128)S(6)} %convert_element_type.131, pred[1024]{0:T(1024)(128)(4,1)S(1)} %iota_compare_fusion.2), kind=kOutput, calls=%fused_computation.8 | convolution fusion | flops 8599371776 | bytes 23069700 | tf_op jit(solution)/shard_map/dot_general | solution.py:102
  374.7 17.3 %psum.7 = f32[1]{0:T(128)} all-reduce(f32[1]{0:T(128)} %bitcast.22), channel_id=1, replica_groups=mesh['dp'=16,'tensor'=8] {'tensor'}, use_global_device_ids=true, to_apply=%region_8.9 | all-reduce | flops 1 | bytes 8 | tf_op jit(solution)/shard_map/psum | solution.py:98
  392.7 83.3 %reduce-scatter.5.cloned.1.call-done = bf16[256,1024]{1,0:T(8,128)(2,1)} async-done(((bf16[4096,1024]{1,0:T(8,128)(2,1)}), bf16[256,1024]{1,0:T(8,128)(2,1)}) %reduce-scatter.5.cloned.1.call-update) | async-done | bytes 524304 | tf_op jit(solution)/shard_map/reduce_scatter | solution.py:101
  476.0 2.1 convert_element_type.134
  (43 shorter events, 5.6 us)
Async XLA Ops:
  7.2 112.6 %copy-start = (bf16[4096,128]{1,0:T(8,128)(2,1)S(1)}, bf16[4096,128]{1,0:T(8,128)(2,1)}, u32[]{:S(2)}) copy-start(bf16[4096,128]{1,0:T(8,128)(2,1)} %param.13) | copy-start | bytes 3145732
  7.2 97.1 %all-gather.3.cloned.1.call-start = ((), (), s32[]{:S(2)}) async-start(), calls=%async_computation.2 | async-start | bytes 9437184 | tf_op jit(solution)/shard_map/all_gather | solution.py:79
  7.9 245.9 %reduce-scatter.3.cloned.1.call-start = ((), (), s32[]{:S(2)}) async-start(), calls=%async_computation.3 | async-start | bytes 9437184 | tf_op jit(solution)/shard_map/reduce_scatter | solution.py:86
  13.0 96.3 %copy-start.7 = (f32[4096]{0:T(1024)S(1)}, f32[4096]{0:T(1024)}, u32[]{:S(2)}) copy-start(f32[4096]{0:T(1024)} %param.10) | copy-start | bytes 49156
  119.7 6.6 %copy-start.2 = (bf16[1024,4096]{1,0:T(8,128)(2,1)S(1)}, bf16[1024,4096]{1,0:T(8,128)(2,1)}, u32[]{:S(2)}) copy-start(bf16[1024,4096]{1,0:T(8,128)(2,1)} %fusion.2) | copy-start | bytes 25165828
  119.7 6.6 %copy-start.6 = (bf16[4096,128]{1,0:T(8,128)(2,1)S(1)}, bf16[4096,128]{1,0:T(8,128)(2,1)}, u32[]{:S(2)}) copy-start(bf16[4096,128]{1,0:T(8,128)(2,1)} %param.12) | copy-start | bytes 3145732
  142.6 2.4 copy-start.5
  145.1 2.1 copy-start.11
  147.2 1.4 copy-start.3
  152.5 2.7 copy-start.9
  162.1 91.7 %copy-start.4 = (bf16[128,4096]{1,0:T(8,128)(2,1)S(1)}, bf16[128,4096]{1,0:T(8,128)(2,1)}, u32[]{:S(2)}) copy-start(bf16[128,4096]{1,0:T(8,128)(2,1)} %param.9) | copy-start | bytes 3145732
  162.1 185.1 %copy-start.10 = (bf16[1024,1024]{1,0:T(8,128)(2,1)S(1)}, bf16[1024,1024]{1,0:T(8,128)(2,1)}, u32[]{:S(2)}) copy-start(bf16[1024,1024]{1,0:T(8,128)(2,1)} %param.16) | copy-start | bytes 6291460
  162.1 185.1 %all-gather.5.cloned.1.call-start = ((), (), s32[]{:S(2)}) async-start(), calls=%async_computation.4 | async-start | bytes 9437184 | tf_op jit(solution)/shard_map/all_gather | solution.py:93
  256.3 219.7 %reduce-scatter.5.cloned.1.call-start = ((), (), s32[]{:S(2)}) async-start(), calls=%async_computation.5 | async-start | bytes 8912896 | tf_op jit(solution)/shard_map/reduce_scatter | solution.py:101
  347.2 15.0 %copy-start.8 = (bf16[1024,4096]{1,0:T(8,128)(2,1)S(1)}, bf16[1024,4096]{1,0:T(8,128)(2,1)}, u32[]{:S(2)}) copy-start(bf16[1024,4096]{1,0:T(8,128)(2,1)} %all-gather.5.cloned.1.call-done) | copy-start | bytes 25165828
  374.6 103.5 %copy-start.1 = (bf16[4096,128]{1,0:T(8,128)(2,1)S(1)}, bf16[4096,128]{1,0:T(8,128)(2,1)}, u32[]{:S(2)}) copy-start(bf16[4096,128]{1,0:T(8,128)(2,1)} %param.13) | copy-start | bytes 3145732
Sparse Core Ops, SparseCore 0:
  9.7 94.5 all-gather.2
  162.3 91.4 reduce-scatter.2
  256.4 90.7 all-gather.4
  374.8 101.1 reduce-scatter.4
where the time goes:
time: 486 us
  waiting for transfers between devices  358 us (74%)
  matrix products  57.5 us (12%)
  other arithmetic  31.5 us (6%)
  blocking collectives  17.3 us (4%)
  between operations  16.4 us (3%)
  local copies, waits for them, and re-layouts  5.04 us (1%)
    reduce_scatter x1, waiting for transfers between devices, shards(): lax.psum_scatter(jnp.dot(attended, w_out, preferred_element_type=jnp.floa...  91.6 us
    all_gather x1, waiting for transfers between devices, shards(): gathered = lax.all_gather(student_in, 'tensor', axis=0, tiled=True)  91.2 us
    all_gather x1, waiting for transfers between devices, shards(): layer = lax.all_gather(own_layer, 'tensor', axis=0, tiled=True)  90.9 us
    reduce_scatter x1, waiting for transfers between devices, shards(): lax.psum_scatter(lax.dot_general(layer, error_grad, (((0,), (0,)), ((), (...  83.3 us
    psum x1, blocking collectives, shards(): squared = lax.psum(jnp.sum(residue * residue), 'tensor')  17.3 us
    dot_general x1, matrix products, shards(): predicted = jnp.dot(layer, projection, preferred_element_type=jnp.float32)  15 us
    dot_general x1, matrix products, shards(): lax.dot_general(layer, error_grad, (((0,), (0,)), ((), ())), preferred_el...  12.4 us
    convert_element_type x1, other arithmetic, root_norm(): (widened * lax.rsqrt(mean_square + EPSILON) * norm_gain).astype(jnp.bfloa...  10.3 us
  transfers between devices with their start and end apart: 4, of which 4 were waited for; matrix products, arithmetic and copies ran while one was open for 1% of the time, Pallas kernels for 0%

commit v1 on v0

v1 whole, which is shorter than its diff:
```python
import math

import jax
import jax.numpy as jnp
from jax import lax
from jax.sharding import Mesh, PartitionSpec as P

HEAD_DIM = 128
DT = 8192
EPSILON = 1e-05
ROPE_BASE = 500000.0
NEG_LARGE = -1e30
AXES = ("x", "yh", "c", "yl", "z")
SIZES = {"x": 4, "yh": 2, "c": 2, "yl": 2, "z": 4}
F32 = jnp.float32
BF16 = jnp.bfloat16


def shift(value, axis, step):
    count = SIZES[axis]
    return lax.ppermute(value, axis, [(i, (i + step) % count) for i in range(count)])


def shift_y(value, step):
    return lax.ppermute(value, ("yh", "yl"), [(i, (i + step) % 4) for i in range(4)])


def after(value, *others):
    return lax.optimization_barrier((value, *others))[0]


def rows_of(array, start, count):
    return lax.dynamic_slice_in_dim(array, start, count, 0)


def dot(left, right):
    return jnp.dot(left, right, preferred_element_type=F32)


def root_norm(inputs, norm_gain):
    widened = inputs.astype(F32)
    mean_square = jnp.mean(widened * widened, axis=-1, keepdims=True)
    return (widened * lax.rsqrt(mean_square + EPSILON) * norm_gain).astype(BF16)


def rotate(values, cosine, sine):
    rows = values.shape[0]
    half = HEAD_DIM // 2
    view = values.reshape(rows, -1, HEAD_DIM)
    lower, upper = view[..., :half], view[..., half:]
    cosine, sine = cosine[:, None, :], sine[:, None, :]
    turned = jnp.concatenate([lower * cosine - upper * sine, upper * cosine + lower * sine], axis=-1)
    return turned.reshape(rows, -1).astype(BF16)


def fetch(plus, minus):
    up, down = shift_y(plus, 1), shift_y(minus, -1)
    return up, down


def swap(pair):
    return tuple(shift(v, "c", 1) for v in pair)


def attend(queries, keys_own, values_own, keys_far, values_far, masks):
    rows = queries.shape[0]
    heads = queries.reshape(rows, 4, HEAD_DIM)
    keys = jnp.concatenate([keys_own, keys_far], axis=0)
    values = jnp.concatenate([values_own, values_far], axis=0)
    scores = jnp.einsum("qgd,kd->gqk", heads, keys, preferred_element_type=F32)
    scores = scores * (1.0 / math.sqrt(HEAD_DIM))
    scores = jnp.where(masks, scores, NEG_LARGE)
    highest = jnp.max(scores, axis=-1, keepdims=True)
    weights = jnp.exp(scores - highest)
    low = (weights / jnp.sum(weights, axis=-1, keepdims=True)).astype(BF16)
    blended = jnp.einsum("gqk,kd->qgd", low, values, preferred_element_type=F32)
    return blended.astype(BF16).reshape(rows, -1)


def shards(
    student_in, norm_gain, w_query, w_key, w_value, w_out, projection, teacher_rows, lengths
):
    x, yh, c, yl, z = (lax.axis_index(a) for a in AXES)
    length = lengths[0]

    normed_own = root_norm(student_in, norm_gain)
    pieces = [normed_own] + [shift(normed_own, "z", -j) for j in (1, 2, 3)]

    kv_own = jnp.concatenate([w_key, w_value], axis=1)
    q_part = lax.dynamic_slice_in_dim(w_query, c * 256, 256, 1)
    kv_part = rows_of(kv_own, c * 2048, 2048)
    first = fetch(
        jnp.concatenate([q_part[:2048], kv_part[:1024]], axis=0),
        jnp.concatenate([q_part[2048:], kv_part[1024:]], axis=0),
    )
    first_sib = swap(first)
    out_part = after(rows_of(w_out, c * 256, 256), *first)
    second = fetch(out_part[:128], out_part[128:])
    second_sib = swap(second)
    proj_view = projection.reshape(8, 2, 256, 1024)
    proj_part = lax.dynamic_index_in_dim(proj_view, c, 1, keepdims=False).reshape(2048, 1024)
    proj_part = after(proj_part, *second)
    third = fetch(proj_part[:1024], proj_part[1024:])
    third_sib = swap(third)
    teach_far = shift(after(rows_of(teacher_rows, (1 - yl) * 512, 512), *third), "yl", 1)

    q_far = jnp.concatenate(
        [
            jnp.concatenate([first[0][:2048], first[1][:2048]], axis=0),
            jnp.concatenate([first_sib[0][:2048], first_sib[1][:2048]], axis=0),
        ],
        axis=1,
    )
    kv_mine = jnp.concatenate([first[0][2048:], first[1][2048:]], axis=0)
    kv_sib = jnp.concatenate([first_sib[0][2048:], first_sib[1][2048:]], axis=0)
    kv_far = jnp.concatenate(
        [jnp.where(c == 0, kv_mine, kv_sib), jnp.where(c == 0, kv_sib, kv_mine)], axis=0
    )
    out_far = jnp.concatenate([*second, *second_sib], axis=0)

    ring = jnp.concatenate([((z + j) % 4) * 128 + jnp.arange(128) for j in range(4)])
    pos = yl * 512 + ring
    pos_far = (1 - yl) * 512 + ring
    inverse = ROPE_BASE ** (-2.0 * jnp.arange(HEAD_DIM // 2).astype(F32) / HEAD_DIM)
    angles = pos.astype(F32)[:, None] * inverse
    cosine, sine = jnp.cos(angles), jnp.sin(angles)
    key_pos = jnp.concatenate([pos, pos_far])
    masks = (pos[:, None] >= key_pos[None, :]) & (key_pos[None, :] < length)

    normed = jnp.concatenate(pieces, axis=0)
    q_own = rotate(dot(normed, w_query), cosine, sine)
    own_kv = dot(normed, kv_own)
    far_kv = dot(normed, kv_far)
    k_own, k_oth = (rotate(v[:, :128], cosine, sine) for v in (own_kv, far_kv))
    v_own, v_oth = (v[:, 128:].astype(BF16) for v in (own_kv, far_kv))
    q_oth = rotate(dot(normed, q_far), cosine, sine)
    sent = shift(jnp.concatenate([k_oth, v_oth, k_own, v_own], axis=1), "yl", 1)
    att_own = attend(q_own, k_own, v_own, sent[:, :128], sent[:, 128:256], masks)
    att_oth = attend(q_oth, k_oth, v_oth, sent[:, 256:384], sent[:, 384:], masks)
    partial = (dot(att_own, w_out) + dot(att_oth, out_far)).astype(BF16)
    blocks = [partial[j * 128 : (j + 1) * 128] for j in range(4)]
    arrived = [blocks[0]] + [shift(blocks[j], "z", j) for j in (1, 2, 3)]
    own_sum = sum(v.astype(F32) for v in arrived)
    own_layer = (student_in.astype(F32) + own_sum).astype(BF16)

    layers = [own_layer] + [shift(own_layer, "z", -j) for j in (1, 2, 3)]
    layer = jnp.concatenate(layers, axis=0)
    split = layer.reshape(512, 8, 2, 256)
    layer_c = lax.dynamic_index_in_dim(split, c, 2, keepdims=False).reshape(512, 2048)
    layer_s = lax.dynamic_index_in_dim(split, 1 - c, 2, keepdims=False).reshape(512, 2048)
    layer_both = jnp.concatenate([layer_c, shift(layer_s, "c", 1)], axis=0)

    def in_ring(array, base):
        return jnp.concatenate(
            [rows_of(array, base + ((z + j) % 4) * 128, 128) for j in range(4)], axis=0
        ).astype(F32)

    live = (pos < length)[:, None]
    scale = length.astype(F32)

    def errors(predicted, teacher):
        residue = jnp.where(live, predicted - teacher, F32(0.0))
        return (residue / scale).astype(BF16), jnp.sum(residue * residue)

    pred_far = dot(layer_c, jnp.concatenate(third, axis=0)) + dot(
        layer_s, jnp.concatenate(third_sib, axis=0)
    )
    err_far, sq_far = errors(pred_far, in_ring(teach_far, 0))
    err_own, sq_own = errors(dot(layer, projection), in_ring(teacher_rows, yl * 512))
    squared = lax.psum(sq_far + sq_own, ("yl", "z"))
    seq_loss = squared.reshape(1) / (lengths.astype(F32) * DT)

    def gradient(error):
        both = jnp.concatenate([error, shift(error, "c", 1)], axis=0)
        return lax.dot_general(
            layer_both, both, (((0,), (0,)), ((), ())), preferred_element_type=F32
        ).astype(BF16)

    grad_far = gradient(err_far).reshape(4, 2, 256, 1024)
    grad_own = gradient(err_own).reshape(4, 2, 256, 1024)
    to_up = jnp.where(yl == 0, yh, 1 - yh)

    def pick(array, at, axis):
        return lax.dynamic_index_in_dim(array, at, axis, keepdims=False)

    def sum_x(array):
        total = pick(array, x, 0).astype(F32)
        for step in (1, 2, 3):
            total = total + shift(pick(array, (x + step) % 4, 0), "x", step).astype(F32)
        return total

    def sum_y(own, far, axis):
        total = pick(own, yh, axis).astype(F32)
        total = total + shift_y(pick(own, 1 - yh, axis), 2).astype(F32)
        total = total + shift_y(pick(far, to_up, axis), 1).astype(F32)
        total = total + shift_y(pick(far, 1 - to_up, axis), -1).astype(F32)
        return total

    a_x = sum_x(
        jnp.concatenate([grad_own[..., :512], grad_far[..., :512]], axis=-1)
    ).astype(BF16)
    b_y = sum_y(grad_own[..., 512:], grad_far[..., 512:], 1).astype(BF16)
    a = sum_y(a_x[..., :512], a_x[..., 512:], 0)
    b = sum_x(b_y)
    return jnp.concatenate([a, b], axis=-1), seq_loss


def solution(mesh):
    split = Mesh(mesh.devices.reshape(4, 2, 2, 2, 4), AXES)
    dp, tensor = ("x", "yh", "c"), ("yl", "z")
    placed = (
        P(dp + tensor, None),
        P(),
        P(None, tensor),
        P(None, tensor),
        P(None, tensor),
        P(tensor, None),
        P(None, tensor),
        P(dp, tensor),
        P(dp),
    )
    return jax.shard_map(
        shards, mesh=split, in_specs=placed, out_specs=(P(dp, tensor), P(dp)), check_vma=False
    )
```

time: 486 us -> 485 us (level); the launches traced: 486 us -> 477 us
  waiting for transfers between devices: 358 us -> 179 us
  local copies, waits for them, and re-layouts: 5.04 us -> 90.3 us
  starting transfers between devices: 0.16 us -> 47.2 us
  matrix products: 57.5 us -> 101 us
  between operations: 16.4 us -> 5.43 us
    all_gather x2 -> x0, waiting for transfers between devices: 182 us -> none  [the longest x1 91.2 us: shards(): gathered = lax.all_gather(student_in, 'tensor', axis=0, tiled=True)]
    ppermute x0 -> x38, waiting for transfers between devices: none -> 179 us  [the longest x26 167 us: shift(): lax.ppermute(value, axis, [(i, (i + step) % count) for i in range(count)])]
    reduce_scatter x2 -> x0, waiting for transfers between devices: 175 us -> none  [the longest x1 91.6 us: shards(): lax.psum_scatter(jnp.dot(attended, w_out, preferred_element_type=jnp.floa...]
    ppermute x0 -> x38, starting transfers between devices: none -> 47.2 us  [the longest x26 27.1 us: shift(): lax.ppermute(value, axis, [(i, (i + step) % count) for i in range(count)])]
    dot_general x10 -> x13, matrix products: 57.5 us -> 87.4 us  [the longest x9 66.1 us: dot(): return jnp.dot(left, right, preferred_element_type=F32)]
    unnamed x26 -> x65, local copies, waits for them, and re-layouts: 3.82 us -> 30.9 us
    slice x1 -> x21, local copies, waits for them, and re-layouts: 1.22 us -> 23.7 us  [the longest x1 2.46 us: shards(): third = fetch(proj_part[:1024], proj_part[1024:])]
    dynamic_slice x0 -> x6, local copies, waits for them, and re-layouts: none -> 22 us  [the longest x1 11.5 us: shards(): lax.dynamic_index_in_dim(split, c, 2, keepdims=False).reshape(512, 2048)]
  transfers between devices with their start and end apart: 4 -> 38, of which waited for: 4 -> 11; matrix products, arithmetic and copies ran while one was open for 1% -> 42% of each run, Pallas kernels for 0% -> 0%
where the time goes in v1:
time: 485 us; the launch traced here: 477 us
  waiting for transfers between devices  179 us (37%)
  matrix products  101 us (21%)
  local copies, waits for them, and re-layouts  90.3 us (19%)
  starting transfers between devices  47.2 us (10%)
  other arithmetic  32.9 us (7%)
  blocking collectives  21 us (4%)
  between operations  5.43 us (1%)
    ppermute x26, waiting for transfers between devices, shift(): lax.ppermute(value, axis, [(i, (i + step) % count) for i in range(count)])  167 us
    dot_general x9, matrix products, dot(): return jnp.dot(left, right, preferred_element_type=F32)  66.1 us
    unnamed x65, local copies, waits for them, and re-layouts  30.9 us
    ppermute x26, starting transfers between devices, shift(): lax.ppermute(value, axis, [(i, (i + step) % count) for i in range(count)])  27.1 us
    psum x1, blocking collectives, shards(): squared = lax.psum(sq_far + sq_own, ('yl', 'z'))  21 us
    ppermute x12, starting transfers between devices, shift_y(): lax.ppermute(value, ('yh', 'yl'), [(i, (i + step) % 4) for i in range(4)])  20.1 us
    sub x2, matrix products, attend(): weights = jnp.exp(scores - highest)  13.7 us
    dot_general x2, matrix products, gradient(): lax.dot_general(layer_both, both, (((0,), (0,)), ((), ())), preferred_ele...  12.7 us
  transfers between devices with their start and end apart: 38, of which 11 were waited for; matrix products, arithmetic and copies ran while one was open for 42% of the time, Pallas kernels for 0%

profile of v1, /device:TPU:0, one launch (start us, length us, event | category | flops | bytes accessed | tf_op | source)
XLA Modules:
  0.0 476.8 jit_solution(10748252633006104959)
XLA Ops:
  29.6 24.5 %collective-permute-done = bf16[128,4096]{1,0:T(8,128)(2,1)} collective-permute-done((bf16[128,4096]{1,0:T(8,128)(2,1)}, bf16[128,4096]{1,0:T(8,128)(2,1)}, u32[]{:S(2)}, u32[]{:S(2)}) %collective-permute-start) | collective-permute-done | bytes 1048608 | tf_op jit(solution)/shard_map/ppermute | solution.py:21
  57.5 6.5 %fusion.118 = f32[512,512]{0,1:T(8,128)S(1)} fusion(bf16[4096,512]{1,0:T(8,128)(2,1)S(1)} %copy-done.12, bf16[128,4096]{1,0:T(8,128)(2,1)} %collective-permute-done.2, bf16[128,4096]{1,0:T(8,128)(2,1)} %collective-permute-done.1, bf16[128,4096]{1,0:T(8,128)(2,1)} %collective-permute-done, bf16[128,4096]{1,0:T(8,128)(2,1)} %fusion.37), kind=kOutput, calls=%fused_computation.211 | convolution fusion | flops 2164260864 | bytes 9437184 | tf_op jit(solution)/shard_map/dot_general | solution.py:37
  70.4 6.1 %fusion.119 = f32[512,256]{0,1:T(8,128)S(1)} fusion(bf16[4096,256]{1,0:T(8,128)(2,1)} %copy-done.11, bf16[128,4096]{1,0:T(8,128)(2,1)} %collective-permute-done.2, bf16[128,4096]{1,0:T(8,128)(2,1)} %collective-permute-done.1, bf16[128,4096]{1,0:T(8,128)(2,1)} %collective-permute-done, bf16[128,4096]{1,0:T(8,128)(2,1)} %fusion.37), kind=kOutput, calls=%fused_computation.212 | convolution fusion | flops 1090519040 | bytes 6815744 | tf_op jit(solution)/shard_map/dot_general | solution.py:37
  81.5 11.4 %collective-permute-done.8 = bf16[128,4096]{1,0:T(8,128)(2,1)} collective-permute-done((bf16[128,4096]{1,0:T(8,128)(2,1)}, bf16[128,4096]{1,0:T(8,128)(2,1)}, u32[]{:S(2)}, u32[]{:S(2)}) %collective-permute-start.8) | collective-permute-done | bytes 1048608 | tf_op jit(solution)/shard_map/ppermute | solution.py:25
  102.0 6.4 %fusion.39 = f32[512,256]{0,1:T(8,128)S(1)} fusion(bf16[2048,256]{1,0:T(8,128)(2,1)S(1)} %get-tuple-element.43, bf16[2048,256]{1,0:T(8,128)(2,1)S(1)} %get-tuple-element.42, bf16[128,4096]{1,0:T(8,128)(2,1)} %collective-permute-done.2, bf16[128,4096]{1,0:T(8,128)(2,1)} %collective-permute-done.1, bf16[128,4096]{1,0:T(8,128)(2,1)} %collective-permute-done, ...), kind=kOutput, calls=%fused_computation.62 | convolution fusion | flops 1094713344 | bytes 6815744 | tf_op jit(solution)/shard_map/dot_general | solution.py:37
  113.4 15.2 %fusion.4 = f32[512,512]{0,1:T(8,128)S(1)} fusion(bf16[2048,256]{1,0:T(8,128)(2,1)S(1)} %slice.191, bf16[2048,256]{1,0:T(8,128)(2,1)S(1)} %slice.190, bf16[2048,256]{1,0:T(8,128)(2,1)S(1)} %slice.189, bf16[2048,256]{1,0:T(8,128)(2,1)S(1)} %slice.188, bf16[128,4096]{1,0:T(8,128)(2,1)} %collective-permute-done.2, ...), kind=kOutput, calls=%fused_computation.20 | convolution fusion | flops 2181038080 | bytes 9437184 | tf_op jit(solution)/shard_map/dot_general | solution.py:37
  136.4 18.6 %collective-permute-done.7 = bf16[512,512]{0,1:T(8,128)(2,1)} collective-permute-done((bf16[512,512]{0,1:T(8,128)(2,1)}, bf16[512,512]{0,1:T(8,128)(2,1)}, u32[]{:S(2)}, u32[]{:S(2)}) %collective-permute-start.7) | collective-permute-done | bytes 524320 | tf_op jit(solution)/shard_map/ppermute | solution.py:21
  156.1 8.1 %fusion.129 = (f32[4,512]{1,0:T(4,128)S(1)}, f32[4,512,1024]{1,2,0:T(8,128)}) fusion(pred[512,1024]{0,1:T(8,128)(4,1)} %compare_and_fusion, bf16[512,128]{0,1:T(8,128)(2,1)S(1)} %get-tuple-element.63, bf16[512,128]{0,1:T(8,128)(2,1)} %copy-done.19, bf16[512,4,64]{2,0,1:T(8,128)(2,1)} %get-tuple-element.65, bf16[512,4,64]{2,0,1:T(8,128)(2,1)} %get-tuple-element.66), kind=kOutput, calls=%fused_computation.222 | convolution fusion | flops 546833408 | bytes 9707520 | tf_op jit(solution)/shard_map/sub | solution.py:74
  168.8 5.8 %fusion.131 = f32[512,4096]{1,0:T(8,128)} fusion(bf16[512,512]{0,1:T(8,128)(2,1)S(1)} %bitcast.140, bf16[512,4096]{1,0:T(8,128)(2,1)S(1)} %copy-done.2), kind=kOutput, calls=%fused_computation.224 | convolution fusion | flops 2147483648 | bytes 13107200 | tf_op jit(solution)/shard_map/dot_general | solution.py:37
  174.6 5.6 %fusion.130 = (f32[4,512]{1,0:T(4,128)S(1)}, f32[4,512,1024]{1,2,0:T(8,128)}) fusion(pred[512,1024]{0,1:T(8,128)(4,1)S(1)} %copy-done.14, bf16[512,128]{0,1:T(8,128)(2,1)S(1)} %get-tuple-element.62, bf16[512,128]{0,1:T(8,128)(2,1)S(1)} %copy-done.18, bf16[512,4,64]{2,0,1:T(8,128)(2,1)S(1)} %copy-done.21, bf16[512,4,64]{2,0,1:T(8,128)(2,1)S(1)} %copy-done.20), kind=kOutput, calls=%fused_computation.223 | convolution fusion | flops 546833408 | bytes 9707520 | tf_op jit(solution)/shard_map/sub | solution.py:74
  198.5 42.2 %collective-permute-done.12 = bf16[128,4096]{1,0:T(8,128)(2,1)} collective-permute-done((bf16[128,4096]{1,0:T(8,128)(2,1)}, bf16[128,4096]{1,0:T(8,128)(2,1)}, u32[]{:S(2)}, u32[]{:S(2)}) %collective-permute-start.12) | collective-permute-done | bytes 1048608 | tf_op jit(solution)/shard_map/ppermute | solution.py:21
  251.3 40.2 %collective-permute-done.15 = bf16[128,4096]{1,0:T(8,128)(2,1)S(1)} collective-permute-done((bf16[128,4096]{1,0:T(8,128)(2,1)S(1)}, bf16[128,4096]{1,0:T(8,128)(2,1)S(1)}, u32[]{:S(2)}, u32[]{:S(2)}) %collective-permute-start.15) | collective-permute-done | bytes 1048608 | tf_op jit(solution)/shard_map/ppermute | solution.py:21
  295.0 5.9 %pad_maximum_fusion.1 = bf16[512,4096]{1,0:T(8,128)(2,1)} fusion(bf16[128,4096]{1,0:T(8,128)(2,1)} %collective-permute-done.17, bf16[128,4096]{1,0:T(8,128)(2,1)} %collective-permute-done.16, bf16[128,4096]{1,0:T(8,128)(2,1)S(1)} %collective-permute-done.15, bf16[128,4096]{1,0:T(8,128)(2,1)S(1)} %fusion.38), kind=kLoop, calls=%fused_computation.35 | loop fusion | flops 16777216 | bytes 8388608 | tf_op jit(solution)/shard_map/concatenate | solution.py:147
  301.0 7.9 %reshape.279 = bf16[512,8,2,256]{3,2,1,0:T(2,128)(2,1)} reshape(bf16[512,4096]{1,0:T(8,128)(2,1)} %pad_maximum_fusion.1) | data formatting | bytes 8388608 | tf_op jit(solution)/shard_map/reshape | solution.py:148
  308.8 11.5 %constant_dynamic-slice_fusion.13 = (bf16[512,8,1,256]{3,2,1,0:T(2,128)(2,1)}, bf16[512,8,1,256]{3,2,1,0:T(2,128)(2,1)}) fusion(bf16[512,8,2,256]{3,2,1,0:T(2,128)(2,1)} %reshape.279, s32[]{:T(128)S(6)} %select_n.172, s32[]{:T(128)S(6)} %select_n.173), kind=kLoop, calls=%fused_computation.177 | loop fusion | bytes 8388616 | tf_op jit(solution)/shard_map/jit(dynamic_index_in_dim)/dynamic_slice | solution.py:149
  320.3 10.6 %copy.40 = bf16[512,8,1,256]{0,3,1,2:T(8,128)(2,1)} copy(bf16[512,8,1,256]{3,2,1,0:T(2,128)(2,1)} %get-tuple-element.20) | data formatting | bytes 4194304
  331.2 11.6 %multiply_reduce_fusion = (f32[]{:T(128)}, bf16[512,1024]{1,0:T(8,128)(2,1)}) fusion(f32[]{:T(128)S(6)} %convert_element_type.182, bf16[128,1024]{1,0:T(8,128)(2,1)S(1)} %copy-done.28, bf16[128,1024]{1,0:T(8,128)(2,1)S(1)} %copy-done.26, bf16[128,1024]{1,0:T(8,128)(2,1)S(1)} %copy-done.27, bf16[128,1024]{1,0:T(8,128)(2,1)S(1)} %copy-done.25, ...), kind=kOutput, calls=%fused_computation.80 | convolution fusion | flops 4319084544 | bytes 14680584 | tf_op jit(solution)/shard_map/dot_general | solution.py:37
  342.7 9.0 %copy.39 = bf16[512,8,1,256]{0,3,1,2:T(8,128)(2,1)S(1)} copy(bf16[512,8,1,256]{3,2,1,0:T(2,128)(2,1)} %get-tuple-element.19) | data formatting | bytes 4194304
  357.1 5.7 %multiply_reduce_fusion.1 = (f32[]{:T(128)}, bf16[512,1024]{1,0:T(8,128)(2,1)S(1)}) fusion(f32[]{:T(128)S(6)} %convert_element_type.182, bf16[128,1024]{1,0:T(8,128)(2,1)S(1)} %copy-done.22, bf16[128,1024]{1,0:T(8,128)(2,1)S(1)} %copy-done.23, bf16[128,1024]{1,0:T(8,128)(2,1)S(1)} %copy-done.24, bf16[128,1024]{1,0:T(8,128)(2,1)S(1)} %get-tuple-element.51, ...), kind=kOutput, calls=%fused_computation.81 | convolution fusion | flops 2163736576 | bytes 10486280 | tf_op jit(solution)/shard_map/dot_general | solution.py:37
  363.6 6.4 %convolution_convert_fusion.1 = bf16[2048,1024]{1,0:T(8,128)(2,1)S(1)} fusion(bf16[512,2048]{0,1:T(8,128)(2,1)} %collective-permute-done.18, bf16[512,2048]{0,1:T(8,128)(2,1)S(1)} %bitcast.135, bf16[512,1024]{1,0:T(8,128)(2,1)S(1)} %collective-permute-done.19, bf16[512,1024]{1,0:T(8,128)(2,1)} %get-tuple-element.31), kind=kOutput, calls=%fused_computation.54 | convolution fusion | flops 4309647360 | bytes 10485760 | tf_op jit(solution)/shard_map/dot_general | solution.py:175
  372.1 6.3 %convolution_convert_fusion = bf16[2048,1024]{1,0:T(8,128)(2,1)S(1)} fusion(bf16[512,2048]{0,1:T(8,128)(2,1)} %collective-permute-done.18, bf16[512,2048]{0,1:T(8,128)(2,1)S(1)} %bitcast.136, bf16[512,1024]{1,0:T(8,128)(2,1)S(1)} %collective-permute-done.25, bf16[512,1024]{1,0:T(8,128)(2,1)S(1)} %get-tuple-element.33), kind=kOutput, calls=%fused_computation.53 | convolution fusion | flops 4309647360 | bytes 10485760 | tf_op jit(solution)/shard_map/dot_general | solution.py:175
  397.1 12.6 %collective-permute-done.26 = bf16[2,256,1024]{2,1,0:T(8,128)(2,1)S(1)} collective-permute-done((bf16[2,256,1024]{2,1,0:T(8,128)(2,1)}, bf16[2,256,1024]{2,1,0:T(8,128)(2,1)S(1)}, u32[]{:S(2)}, u32[]{:S(2)}) %collective-permute-start.26) | collective-permute-done | bytes 1048608 | tf_op jit(solution)/shard_map/ppermute | solution.py:21
  411.7 21.5 %collective-permute-done.27 = bf16[2,256,1024]{2,1,0:T(8,128)(2,1)} collective-permute-done((bf16[2,256,1024]{2,1,0:T(8,128)(2,1)}, bf16[2,256,1024]{2,1,0:T(8,128)(2,1)}, u32[]{:S(2)}, u32[]{:S(2)}) %collective-permute-start.27) | collective-permute-done | bytes 1048608 | tf_op jit(solution)/shard_map/ppermute | solution.py:21
  450.1 21.0 %psum.7 = f32[1]{0:T(128)} all-reduce(f32[1]{0:T(128)} %bitcast.39), channel_id=1, replica_groups=mesh['x'=4,'yh'=2,'c'=2,'yl'=2,'z'=4] {'yl','z'}, use_global_device_ids=true, to_apply=%region_7.8 | all-reduce | flops 1 | bytes 8 | tf_op jit(solution)/shard_map/psum | solution.py:170
  (198 shorter events, 150.8 us)
Async XLA Ops:
  4.8 49.3 %collective-permute-start = (bf16[128,4096]{1,0:T(8,128)(2,1)}, bf16[128,4096]{1,0:T(8,128)(2,1)}, u32[]{:S(2)}, u32[]{:S(2)}) collective-permute-start(bf16[128,4096]{1,0:T(8,128)(2,1)} %fusion.37), channel_id=1, source_target_pairs={{0,3},{1,0},{2,1},{3,2},{4,7},{5,4},{6,5},{7,6},{8,11},{9,8},{10,9... | collective-permute-start | bytes 3145736 | tf_op jit(solution)/shard_map/ppermute | solution.py:21
  8.9 45.2 %collective-permute-start.1 = (bf16[128,4096]{1,0:T(8,128)(2,1)}, bf16[128,4096]{1,0:T(8,128)(2,1)}, u32[]{:S(2)}, u32[]{:S(2)}) collective-permute-start(bf16[128,4096]{1,0:T(8,128)(2,1)} %fusion.37), channel_id=1, source_target_pairs={{0,2},{1,3},{2,0},{3,1},{4,6},{5,7},{6,4},{7,5},{8,10},{9,11},{10,... | collective-permute-start | bytes 3145736 | tf_op jit(solution)/shard_map/ppermute | solution.py:21
  8.9 48.6 %collective-permute-start.2 = (bf16[128,4096]{1,0:T(8,128)(2,1)}, bf16[128,4096]{1,0:T(8,128)(2,1)}, u32[]{:S(2)}, u32[]{:S(2)}) collective-permute-start(bf16[128,4096]{1,0:T(8,128)(2,1)} %fusion.37), channel_id=1, source_target_pairs={{0,1},{1,2},{2,3},{3,0},{4,5},{5,6},{6,7},{7,4},{8,9},{9,10},{10,1... | collective-permute-start | bytes 3145736 | tf_op jit(solution)/shard_map/ppermute | solution.py:21
  15.6 48.4 %collective-permute-start.3 = (bf16[3072,256]{1,0:T(8,128)(2,1)}, bf16[3072,256]{1,0:T(8,128)(2,1)}, u32[]{:S(2)}, u32[]{:S(2)}) collective-permute-start(bf16[3072,256]{1,0:T(8,128)(2,1)} %pad_maximum_fusion.5), channel_id=1, source_target_pairs={{0,4},{4,16},{16,20},{20,0},{1,5},{5,17},{17,21},{21,1},{2,6},{6,1... | collective-permute-start | bytes 4718600 | tf_op jit(solution)/shard_map/ppermute | solution.py:25
  17.3 46.7 %collective-permute-start.4 = (bf16[3072,256]{1,0:T(8,128)(2,1)S(1)}, bf16[3072,256]{1,0:T(8,128)(2,1)}, u32[]{:S(2)}, u32[]{:S(2)}) collective-permute-start(bf16[3072,256]{1,0:T(8,128)(2,1)S(1)} %pad_maximum_fusion.6), channel_id=1, source_target_pairs={{0,20},{4,0},{16,4},{20,16},{1,21},{5,1},{17,5},{21,17},{2,22},{6,... | collective-permute-start | bytes 4718600 | tf_op jit(solution)/shard_map/ppermute | solution.py:25
  64.2 36.3 %collective-permute-start.6 = (bf16[3072,256]{1,0:T(8,128)(2,1)}, bf16[3072,256]{1,0:T(8,128)(2,1)}, u32[]{:S(2)}, u32[]{:S(2)}) collective-permute-start(bf16[3072,256]{1,0:T(8,128)(2,1)} %collective-permute-done.4), channel_id=1, source_target_pairs={{0,8},{8,0},{1,9},{9,1},{2,10},{10,2},{3,11},{11,3},{4,12},{12,4},... | collective-permute-start | bytes 4718600 | tf_op jit(solution)/shard_map/ppermute | solution.py:21
  95.7 102.5 %collective-permute-start.20 = (bf16[1024,1024]{1,0:T(8,128)(2,1)}, bf16[1024,1024]{1,0:T(8,128)(2,1)}, u32[]{:S(2)}, u32[]{:S(2)}) collective-permute-start(bf16[1024,1024]{1,0:T(8,128)(2,1)} %get-tuple-element.17), channel_id=1, source_target_pairs={{0,4},{4,16},{16,20},{20,0},{1,5},{5,17},{17,21},{21,1},{2,6},{6,1... | collective-permute-start | bytes 6291464 | tf_op jit(solution)/shard_map/ppermute | solution.py:25
  97.2 101.0 %collective-permute-start.21 = (bf16[1024,1024]{1,0:T(8,128)(2,1)}, bf16[1024,1024]{1,0:T(8,128)(2,1)}, u32[]{:S(2)}, u32[]{:S(2)}) collective-permute-start(bf16[1024,1024]{1,0:T(8,128)(2,1)} %get-tuple-element.18), channel_id=1, source_target_pairs={{0,20},{4,0},{16,4},{20,16},{1,21},{5,1},{17,5},{21,17},{2,22},{6,... | collective-permute-start | bytes 6291464 | tf_op jit(solution)/shard_map/ppermute | solution.py:25
  98.9 85.5 %collective-permute-start.10 = (bf16[128,4096]{1,0:T(8,128)(2,1)}, bf16[128,4096]{1,0:T(8,128)(2,1)}, u32[]{:S(2)}, u32[]{:S(2)}) collective-permute-start(bf16[128,4096]{1,0:T(8,128)(2,1)} %collective-permute-done.8), channel_id=1, source_target_pairs={{0,8},{8,0},{1,9},{9,1},{2,10},{10,2},{3,11},{11,3},{4,12},{12,4},... | collective-permute-start | bytes 3145736 | tf_op jit(solution)/shard_map/ppermute | solution.py:21
  98.9 85.6 %collective-permute-start.11 = (bf16[128,4096]{1,0:T(8,128)(2,1)}, bf16[128,4096]{1,0:T(8,128)(2,1)}, u32[]{:S(2)}, u32[]{:S(2)}) collective-permute-start(bf16[128,4096]{1,0:T(8,128)(2,1)} %collective-permute-done.9), channel_id=1, source_target_pairs={{0,8},{8,0},{1,9},{9,1},{2,10},{10,2},{3,11},{11,3},{4,12},{12,4},... | collective-permute-start | bytes 3145736 | tf_op jit(solution)/shard_map/ppermute | solution.py:21
  110.0 44.9 %collective-permute-start.7 = (bf16[512,512]{0,1:T(8,128)(2,1)}, bf16[512,512]{0,1:T(8,128)(2,1)}, u32[]{:S(2)}, u32[]{:S(2)}) collective-permute-start(bf16[512,512]{0,1:T(8,128)(2,1)} %pad_maximum_fusion.10), channel_id=1, source_target_pairs={{0,4},{4,0},{1,5},{5,1},{2,6},{6,2},{3,7},{7,3},{8,12},{12,8},{9,1... | collective-permute-start | bytes 1572872 | tf_op jit(solution)/shard_map/ppermute | solution.py:21
  193.9 46.8 %collective-permute-start.12 = (bf16[128,4096]{1,0:T(8,128)(2,1)}, bf16[128,4096]{1,0:T(8,128)(2,1)}, u32[]{:S(2)}, u32[]{:S(2)}) collective-permute-start(bf16[128,4096]{1,0:T(8,128)(2,1)} %get-tuple-element.21), channel_id=1, source_target_pairs={{0,1},{1,2},{2,3},{3,0},{4,5},{5,6},{6,7},{7,4},{8,9},{9,10},{10,1... | collective-permute-start | bytes 3145736 | tf_op jit(solution)/shard_map/ppermute | solution.py:21
  193.9 46.8 %collective-permute-start.13 = (bf16[128,4096]{1,0:T(8,128)(2,1)}, bf16[128,4096]{1,0:T(8,128)(2,1)}, u32[]{:S(2)}, u32[]{:S(2)}) collective-permute-start(bf16[128,4096]{1,0:T(8,128)(2,1)} %get-tuple-element.23), channel_id=1, source_target_pairs={{0,2},{1,3},{2,0},{3,1},{4,6},{5,7},{6,4},{7,5},{8,10},{9,11},{10,... | collective-permute-start | bytes 3145736 | tf_op jit(solution)/shard_map/ppermute | solution.py:21
  196.3 45.1 %collective-permute-start.14 = (bf16[128,4096]{1,0:T(8,128)(2,1)}, bf16[128,4096]{1,0:T(8,128)(2,1)}, u32[]{:S(2)}, u32[]{:S(2)}) collective-permute-start(bf16[128,4096]{1,0:T(8,128)(2,1)} %get-tuple-element.22), channel_id=1, source_target_pairs={{0,3},{1,0},{2,1},{3,2},{4,7},{5,4},{6,5},{7,6},{8,11},{9,8},{10,9... | collective-permute-start | bytes 3145736 | tf_op jit(solution)/shard_map/ppermute | solution.py:21
  198.2 51.7 %collective-permute-start.24 = (bf16[512,1024]{1,0:T(8,128)(2,1)}, bf16[512,1024]{1,0:T(8,128)(2,1)S(1)}, u32[]{:S(2)}, u32[]{:S(2)}) collective-permute-start(bf16[512,1024]{1,0:T(8,128)(2,1)} %constant_dynamic-slice_fusion.6), channel_id=1, source_target_pairs={{0,4},{4,0},{1,5},{5,1},{2,6},{6,2},{3,7},{7,3},{8,12},{12,8},{9,1... | collective-permute-start | bytes 3145736 | tf_op jit(solution)/shard_map/ppermute | solution.py:21
  244.3 47.1 %collective-permute-start.15 = (bf16[128,4096]{1,0:T(8,128)(2,1)S(1)}, bf16[128,4096]{1,0:T(8,128)(2,1)S(1)}, u32[]{:S(2)}, u32[]{:S(2)}) collective-permute-start(bf16[128,4096]{1,0:T(8,128)(2,1)S(1)} %fusion.38), channel_id=1, source_target_pairs={{0,3},{1,0},{2,1},{3,2},{4,7},{5,4},{6,5},{7,6},{8,11},{9,8},{10,9... | collective-permute-start | bytes 3145736 | tf_op jit(solution)/shard_map/ppermute | solution.py:21
  246.8 44.7 %collective-permute-start.16 = (bf16[128,4096]{1,0:T(8,128)(2,1)S(1)}, bf16[128,4096]{1,0:T(8,128)(2,1)}, u32[]{:S(2)}, u32[]{:S(2)}) collective-permute-start(bf16[128,4096]{1,0:T(8,128)(2,1)S(1)} %fusion.38), channel_id=1, source_target_pairs={{0,2},{1,3},{2,0},{3,1},{4,6},{5,7},{6,4},{7,5},{8,10},{9,11},{10,... | collective-permute-start | bytes 3145736 | tf_op jit(solution)/shard_map/ppermute | solution.py:21
  246.8 48.3 %collective-permute-start.17 = (bf16[128,4096]{1,0:T(8,128)(2,1)S(1)}, bf16[128,4096]{1,0:T(8,128)(2,1)}, u32[]{:S(2)}, u32[]{:S(2)}) collective-permute-start(bf16[128,4096]{1,0:T(8,128)(2,1)S(1)} %fusion.38), channel_id=1, source_target_pairs={{0,1},{1,2},{2,3},{3,0},{4,5},{5,6},{6,7},{7,4},{8,9},{9,10},{10,1... | collective-permute-start | bytes 3145736 | tf_op jit(solution)/shard_map/ppermute | solution.py:21
  249.9 107.2 %collective-permute-start.22 = (bf16[1024,1024]{1,0:T(8,128)(2,1)}, bf16[1024,1024]{1,0:T(8,128)(2,1)}, u32[]{:S(2)}, u32[]{:S(2)}) collective-permute-start(bf16[1024,1024]{1,0:T(8,128)(2,1)} %collective-permute-done.20), channel_id=1, source_target_pairs={{0,8},{8,0},{1,9},{9,1},{2,10},{10,2},{3,11},{11,3},{4,12},{12,4},... | collective-permute-start | bytes 6291464 | tf_op jit(solution)/shard_map/ppermute | solution.py:21
  249.9 107.2 %collective-permute-start.23 = (bf16[1024,1024]{1,0:T(8,128)(2,1)}, bf16[1024,1024]{1,0:T(8,128)(2,1)}, u32[]{:S(2)}, u32[]{:S(2)}) collective-permute-start(bf16[1024,1024]{1,0:T(8,128)(2,1)} %collective-permute-done.21), channel_id=1, source_target_pairs={{0,8},{8,0},{1,9},{9,1},{2,10},{10,2},{3,11},{11,3},{4,12},{12,4},... | collective-permute-start | bytes 6291464 | tf_op jit(solution)/shard_map/ppermute | solution.py:21
  384.7 48.6 %collective-permute-start.27 = (bf16[2,256,1024]{2,1,0:T(8,128)(2,1)}, bf16[2,256,1024]{2,1,0:T(8,128)(2,1)}, u32[]{:S(2)}, u32[]{:S(2)}) collective-permute-start(bf16[2,256,1024]{2,1,0:T(8,128)(2,1)} %get-tuple-element.11), channel_id=1, source_target_pairs={{0,64},{32,96},{64,0},{96,32},{1,65},{33,97},{65,1},{97,33},{2,66}... | collective-permute-start | bytes 3145736 | tf_op jit(solution)/shard_map/ppermute | solution.py:21
  387.4 45.9 %collective-permute-start.28 = (bf16[2,256,1024]{2,1,0:T(8,128)(2,1)}, bf16[2,256,1024]{2,1,0:T(8,128)(2,1)}, u32[]{:S(2)}, u32[]{:S(2)}) collective-permute-start(bf16[2,256,1024]{2,1,0:T(8,128)(2,1)} %get-tuple-element.12), channel_id=1, source_target_pairs={{0,96},{32,0},{64,32},{96,64},{1,97},{33,1},{65,33},{97,65},{2,98}... | collective-permute-start | bytes 3145736 | tf_op jit(solution)/shard_map/ppermute | solution.py:21
  391.1 48.2 %collective-permute-start.32 = (bf16[4,256,512]{2,1,0:T(8,128)(2,1)}, bf16[4,256,512]{2,1,0:T(8,128)(2,1)}, u32[]{:S(2)}, u32[]{:S(2)}) collective-permute-start(bf16[4,256,512]{2,1,0:T(8,128)(2,1)} %dynamic-slice_bitcast_fusion.2), channel_id=1, source_target_pairs={{0,16},{4,20},{16,0},{20,4},{1,17},{5,21},{17,1},{21,5},{2,18},{6,... | collective-permute-start | bytes 3145736 | tf_op jit(solution)/shard_map/ppermute | solution.py:25
  397.1 44.0 %collective-permute-start.33 = (bf16[4,256,512]{2,1,0:T(8,128)(2,1)}, bf16[4,256,512]{2,1,0:T(8,128)(2,1)}, u32[]{:S(2)}, u32[]{:S(2)}) collective-permute-start(bf16[4,256,512]{2,1,0:T(8,128)(2,1)} %get-tuple-element.38), channel_id=1, source_target_pairs={{0,4},{4,16},{16,20},{20,0},{1,5},{5,17},{17,21},{21,1},{2,6},{6,1... | collective-permute-start | bytes 3145736 | tf_op jit(solution)/shard_map/ppermute | solution.py:25
  (43 other events, 684.7 us)
